TPU v7x, 32 devices: a whole 2x2x4 slice. The times are simulated.
32 devices in a mesh: pp: 2 (over y), fsdp: 8 (over z, x), tp: 2 (over core).
Axes of the slice: x: 2, y: 2, z: 4, core: 2. Of those that a mesh axis runs over, the one named last changes fastest.
Arguments:
- saved_inputs: bfloat16 [2, 1024, 8192], P('pp', 'fsdp', 'tp'), may hold values from -6 to 6
- returned: bfloat16 [2, 1024, 8192], P('pp', 'fsdp', 'tp'), may hold values from -6 to 6
- proj_weight: bfloat16 [2, 8192, 640], P('pp', 'tp', 'fsdp'), may hold values from -0.03125 to 0.03125
- log_rate: float32 [2, 128], P('pp', 'tp'), may hold values from -4.6 to -1.2
- step_bias: float32 [2, 128], P('pp', 'tp'), may hold values from -3 to -1
- skip_gain: float32 [2, 128], P('pp', 'tp'), may hold values from 0.5 to 1.5
Outputs:
- grad_out: bfloat16 [2, 1024, 8192], P('pp', 'fsdp', 'tp')
- weight_grad: float32 [2, 8192, 640], P('pp', 'tp', 'fsdp')
All inputs are finite; a program needn't handle non-finite values.
Results may differ from a plain program's by a relative error of at most 0.0044.
Values may be sent and summed in bfloat16 or wider, within the bound.
A program may use at most 64 MiB of HBM per device.

v0:
```python
import jax
import jax.numpy as jnp
from jax import lax
from jax.sharding import PartitionSpec as P

HEAD_DIM = 64
STATE = 256
BLOCK = 128


def shifted(value, axis, by):
    count = lax.axis_size(axis)
    return lax.ppermute(value, axis, [(i, (i + by) % count) for i in range(count)])


def state_space(head_input, b_values, c_values, raw_step, log_rate, step_bias, skip_gain):
    length, head_count, head_size = head_input.shape
    blocks = length // BLOCK
    highest = lax.Precision.HIGHEST
    step_size = jax.nn.softplus(raw_step + step_bias[None, :])
    log_decay = -step_size * jnp.exp(log_rate)[None, :]
    block_values = head_input.reshape(blocks, BLOCK, head_count, head_size)
    b_blocks = b_values.reshape(blocks, BLOCK, b_values.shape[1])
    c_blocks = c_values.reshape(blocks, BLOCK, c_values.shape[1])
    cumulative = jnp.cumsum(log_decay.reshape(blocks, BLOCK, head_count), axis=1)
    scaled = block_values * step_size.reshape(blocks, BLOCK, head_count)[..., None]
    scores = jnp.einsum("kin,kjn->kij", c_blocks, b_blocks, precision=highest)
    causal = (jnp.arange(BLOCK)[:, None] >= jnp.arange(BLOCK)[None, :])[None, :, :, None]
    log_gaps = cumulative[:, :, None, :] - cumulative[:, None, :, :]
    mixing = jnp.where(causal, jnp.exp(jnp.where(causal, log_gaps, 0.0)), 0.0) * scores[..., None]
    within = jnp.einsum("kijh,kjhp->kihp", mixing, scaled, precision=highest)
    to_end = jnp.exp(cumulative[:, -1:, :] - cumulative)
    states = jnp.einsum("kjn,kjhp->khnp", b_blocks, scaled * to_end[..., None], precision=highest)
    totals = jnp.exp(cumulative[:, -1, :])

    def advance(running, inputs_pair):
        block_state, block_total = inputs_pair
        return (block_total[:, None, None] * running + block_state, running)

    start_state = jnp.zeros((head_count, b_values.shape[1], head_size), head_input.dtype)
    _, entering = lax.scan(advance, start_state, (states, totals))
    across = (
        jnp.einsum("kin,khnp->kihp", c_blocks, entering, precision=highest)
        * jnp.exp(cumulative)[..., None]
    )
    output = (within + across).reshape(length, head_count, head_size)
    return output + skip_gain[None, :, None] * head_input


def head_share(partial_sums):
    return lax.psum_scatter(partial_sums, "tp", scatter_dimension=0, tiled=True)


def per_device(saved_inputs, returned, proj_weight, log_rate, step_bias, skip_gain):
    inputs = saved_inputs[0]
    row_count, inner_here = inputs.shape
    heads_here = log_rate.shape[1]
    weight_local = proj_weight[0]
    arrived = shifted(returned, "pp", -1)[0]
    weight_full = lax.all_gather(weight_local, "fsdp", axis=1, tiled=True)
    partial_proj = jnp.dot(inputs, weight_full, preferred_element_type=jnp.float32)
    projected = lax.all_gather(head_share(partial_proj), "tp", axis=0, tiled=True)
    head_total = projected.shape[1] - 2 * STATE
    offset = lax.axis_index("tp") * heads_here
    raw_step = lax.dynamic_slice_in_dim(projected, 2 * STATE + offset, heads_here, 1)
    values = inputs.astype(jnp.float32).reshape(row_count, heads_here, HEAD_DIM)

    def local_core(head_input, b_values, c_values, step_raw):
        return state_space(
            head_input, b_values, c_values, step_raw, log_rate[0], step_bias[0], skip_gain[0]
        )

    _, backward = jax.vjp(
        local_core, values, projected[:, :STATE], projected[:, STATE : 2 * STATE], raw_step
    )
    upstream = arrived.astype(jnp.float32)
    grad_x, grad_b, grad_c, grad_raw = backward(upstream.reshape(row_count, heads_here, HEAD_DIM))
    placed = lax.dynamic_update_slice_in_dim(
        jnp.zeros((row_count, head_total), jnp.float32), grad_raw, offset, 1
    )
    grad_share = head_share(jnp.concatenate([grad_b, grad_c, placed], axis=1)).astype(jnp.bfloat16)
    proj_grad = lax.all_gather(grad_share, "tp", axis=0, tiled=True)
    back_proj = lax.dot_general(
        proj_grad, weight_full, (((1,), (1,)), ((), ())), preferred_element_type=jnp.float32
    )
    grad_inputs = (upstream + grad_x.reshape(row_count, inner_here) + back_proj).astype(
        jnp.bfloat16
    )
    share = lax.psum_scatter(
        lax.dot_general(
            proj_grad, inputs, (((0,), (0,)), ((), ())), preferred_element_type=jnp.float32
        ),
        "fsdp",
        scatter_dimension=0,
        tiled=True,
    )
    section_wgrad = share.T
    return (grad_inputs[None], section_wgrad[None])


def solution(mesh):
    placed = (
        P("pp", "fsdp", "tp"),
        P("pp", "fsdp", "tp"),
        P("pp", "tp", "fsdp"),
        P("pp", "tp"),
        P("pp", "tp"),
        P("pp", "tp"),
    )
    return jax.shard_map(
        per_device,
        mesh=mesh,
        in_specs=placed,
        out_specs=(P("pp", "fsdp", "tp"), P("pp", "tp", "fsdp")),
        check_vma=False,
    )
```

profile of v0, /device:TPU:0, one launch (start us, length us, event | category | flops | bytes accessed | tf_op | source)
XLA Modules:
  0.0 382.9 jit_solution(1650679769397168504)
XLA Ops:
  7.2 0.7 all-gather.3.cloned.1.call-update
  8.0 3.0 collective-permute-start
  11.0 88.2 %all-gather.3.cloned.1.call-done = bf16[1,4096,640]{1,2,0:T(8,128)(2,1)} async-done(((bf16[1,4096,80]{1,2,0:T(8,128)(2,1)}), bf16[1,4096,640]{1,2,0:T(8,128)(2,1)}) %all-gather.3.cloned.1.call-update) | async-done | bytes 5242896 | tf_op jit(solution)/shard_map/all_gather | solution.py:60
  99.2 5.3 %fusion.2 = f32[128,640]{1,0:T(8,128)} fusion(bf16[1,4096,640]{1,2,0:T(8,128)(2,1)} %all-gather.3.cloned.1.call-done, bf16[1,128,4096]{2,1,0:T(8,128)(2,1)} %param.6), kind=kOutput, calls=%fused_computation.2 | convolution fusion | flops 671088640 | bytes 6619136 | tf_op jit(solution)/shard_map/dot_general | solution.py:61
  104.6 0.7 copy.83
  105.3 0.7 copy.79
  106.0 1.4 convert_element_type.57
  107.4 0.6 exponential_bitcast_fusion
  108.0 1.3 copy.80
  109.3 1.7 copy.90
  111.0 2.2 all_gather.10
  113.2 0.9 fusion.57
  114.1 1.4 multiply_bitcast_fusion
  115.5 1.6 reduce_window_sum.26
  117.1 1.2 exponential_multiply_fusion
  118.3 1.5 copy.78
  119.9 4.8 %fusion.17 = f32[128,4096]{0,1} fusion(f32[128,640]{1,0:T(8,128)S(1)} %all_gather.10), kind=kOutput, calls=%fused_computation.23 | convolution fusion | flops 1610612736 | bytes 2228224
  124.7 4.7 %fusion.32 = f32[64,64,128]{2,1,0:T(8,128)} fusion(f32[128,640]{1,0:T(8,128)S(1)} %all_gather.10), kind=kOutput, calls=%fused_computation.44 | convolution fusion | flops 1610612736 | bytes 2228224 | tf_op jit(solution)/shard_map/transpose(jvp(kjn,kjhp->khnp))/dot_general | solution.py:33
  129.4 1.6 copy.93
  131.0 0.7 copy.81
  131.7 1.5 bitcast_exponential_fusion
  133.2 2.3 bitcast_multiply_fusion.4
  135.5 6.9 %fusion.16 = (f32[128,64]{0,1:T(8,128)S(1)}, f32[128,64]{0,1:T(8,128)}, f32[1,128,64,64]{1,3,2,0:T(8,128)}) fusion(f32[64,64,128]{2,1,0:T(8,128)} %fusion.32, f32[1,128,64,64]{1,3,2,0:T(8,128)S(1)} %bitcast.152, f32[128,64]{0,1:T(8,128)S(1)} %copy-done.8, bf16[64,64,128]{2,1,0:T(8,128)(2,1)S(1)} %bitcast.156, f32[128,128]{1,0:T(8,128)S(1)} %copy-done.6, ...), kind=kOutput, calls=%fused_computation.22 | convolution fusion | flops 813678592 | bytes 7585792 | tf_op jit(solution)/shard_map/transpose(jvp(kijh,kjhp->kihp))/dot_general | solution.py:31
  142.4 0.7 multiply_reduce_fusion.2
  143.1 0.7 copy.92
  143.8 1.5 mul.223
  145.3 2.9 copy.86
  148.2 3.1 convert_multiply_fusion
  151.4 3.0 copy.87
  154.4 5.1 %fusion.40 = f32[128,256]{0,1:T(8,128)S(1)} fusion(f32[128,64,64]{0,2,1:T(8,128)} %bitcast.151), kind=kOutput, calls=%fused_computation.50 | convolution fusion | flops 1610612736 | bytes 2228224 | tf_op jit(solution)/shard_map/transpose(jvp(kin,khnp->kihp))/dot_general | solution.py:43
  159.6 7.3 %fusion.15 = (f32[128,64]{0,1:T(8,128)}, f32[128,64]{0,1:T(8,128)}, f32[128,128]{0,1:T(8,128)S(1)}) fusion(f32[128,128]{0,1:T(8,128)S(1)} %copy-done.13, f32[128,64]{0,1:T(8,128)S(1)} %bitcast.159, pred[128,128]{0,1:T(8,128)(4,1)S(1)} %iota_compare_fusion, bf16[64,64,128]{2,1,0:T(8,128)(2,1)S(1)} %bitcast.157, f32[128,64,64]{0,2,1:T(8,128)S(1)} %bitcast.153, ...), kind=kOutput, calls=%fused_computation.18 | convolution fusion | flops 817332224 | bytes 3424256 | tf_op jit(solution)/shard_map/transpose(jvp(kijh,kjhp->kihp))/dot_general | solution.py:31
  166.8 0.4 convolution_bitcast_fusion
  167.2 0.4 convolution_add_fusion
  167.6 0.8 copy.94
  168.5 0.9 copy.95
  169.4 2.8 multiply_reduce_fusion
  172.6 1.1 reduce_window_sum.29
  173.7 0.1 fusion.64
  173.9 5.1 %fusion.46 = f32[128,256]{0,1:T(8,128)S(1)} fusion(f32[1,128,256]{1,2,0:T(8,128)S(1)} %convolution_bitcast_fusion, f32[128,64,64]{0,2,1:T(8,128)} %bitcast.155), kind=kOutput, calls=%fused_computation.52 | convolution fusion | flops 1610645504 | bytes 2359296 | tf_op jit(solution)/shard_map/transpose(jvp(kjn,kjhp->khnp))/dot_general | solution.py:33
  179.0 0.9 copy.103
  180.0 8.6 %reduce-scatter.10.cloned.1.call-done = f32[64,640]{1,0:T(8,128)} async-done(((f32[128,640]{1,0:T(8,128)}), f32[64,640]{1,0:T(8,128)}) %reduce-scatter.10.cloned.1.call-update) | async-done | bytes 163856 | tf_op jit(solution)/shard_map/reduce_scatter | solution.py:51
  188.5 0.9 convert_element_type.65
  189.5 1.9 all_gather.11
  191.4 5.5 %fusion.50 = f32[640,4096]{1,0:T(8,128)} fusion(bf16[128,640]{1,0:T(8,128)(2,1)S(1)} %all_gather.11, bf16[1,128,4096]{2,1,0:T(8,128)(2,1)S(1)} %copy-done), kind=kOutput, calls=%fused_computation.54 | convolution fusion | flops 671088640 | bytes 11698176 | tf_op jit(solution)/shard_map/dot_general | solution.py:90
  196.9 0.6 copy-done.20
  197.7 1.9 copy.82
  199.6 4.6 %fusion.49 = bf16[1,128,4096]{2,1,0:T(8,128)(2,1)} fusion(f32[128,4096]{1,0:T(8,128)S(1)} %copy.82, bf16[1,128,4096]{2,1,0:T(8,128)(2,1)S(1)} %collective-permute-done, f32[4096]{0:T(1024)S(1)} %mul.201, bf16[128,640]{1,0:T(8,128)(2,1)S(1)} %all_gather.11, bf16[1,4096,640]{1,2,0:T(8,128)(2,1)} %all-gather.3.cloned.1.call-done), kind=kOutput, calls=%fused_computation.53 | convolution fusion | flops 674234368 | bytes 9617408 | tf_op jit(solution)/shard_map/dot_general | solution.py:83
  204.2 172.1 %reduce-scatter.8.cloned.1.call-done = f32[80,4096]{1,0:T(8,128)} async-done(((f32[640,4096]{1,0:T(8,128)}), f32[80,4096]{1,0:T(8,128)}) %reduce-scatter.8.cloned.1.call-update) | async-done | bytes 1310736 | tf_op jit(solution)/shard_map/reduce_scatter | solution.py:89
  (64 shorter events, 0.8 us)
Async XLA Ops:
  7.2 92.0 %all-gather.3.cloned.1.call-start = ((), (), s32[]{:S(2)}) async-start(), calls=%async_computation.5 | async-start | bytes 5898240 | tf_op jit(solution)/shard_map/all_gather | solution.py:60
  7.9 96.7 %copy-start = (bf16[1,128,4096]{2,1,0:T(8,128)(2,1)S(1)}, bf16[1,128,4096]{2,1,0:T(8,128)(2,1)}, u32[]{:S(2)}) copy-start(bf16[1,128,4096]{2,1,0:T(8,128)(2,1)} %param.6) | copy-start | bytes 3145732
  7.9 103.1 %reduce-scatter.6.cloned.1.call-start = ((), (), s32[]{:S(2)}) async-start(), calls=%async_computation.3 | async-start | bytes 491520 | tf_op jit(solution)/shard_map/reduce_scatter | solution.py:51
  8.0 100.1 %collective-permute-start = (bf16[1,128,4096]{2,1,0:T(8,128)(2,1)}, bf16[1,128,4096]{2,1,0:T(8,128)(2,1)S(1)}, u32[]{:S(2)}, u32[]{:S(2)}) collective-permute-start(bf16[1,128,4096]{2,1,0:T(8,128)(2,1)} %param.7), channel_id=1, source_target_pairs={{0,16},{16,0},{1,17},{17,1},{2,18},{18,2},{3,19},{19,3},{4,20},{20... | collective-permute-start | bytes 3145736 | tf_op jit(solution)/shard_map/ppermute | solution.py:13
  104.5 84.0 %reduce-scatter.10.cloned.1.call-start = ((), (), s32[]{:S(2)}) async-start(), calls=%async_computation.6 | async-start | bytes 491520 | tf_op jit(solution)/shard_map/reduce_scatter | solution.py:51
  105.2 2.2 copy-start.22
  131.6 3.8 %copy-start.1 = (f32[1,128,4096]{1,2,0:T(8,128)S(1)}, f32[1,128,4096]{1,2,0:T(8,128)}, u32[]{:S(2)}) copy-start(f32[1,128,4096]{1,2,0:T(8,128)} %convert_element_type.57) | copy-start | bytes 6291460
  131.6 3.8 %copy-start.3 = (bf16[1,128,4096]{1,2,0:T(8,128)(2,1)S(1)}, bf16[1,128,4096]{1,2,0:T(8,128)(2,1)}, u32[]{:S(2)}) copy-start(bf16[1,128,4096]{1,2,0:T(8,128)(2,1)} %copy.80) | copy-start | bytes 3145732
  131.6 3.8 %copy-start.6 = (f32[128,128]{1,0:T(8,128)S(1)}, f32[128,128]{1,0:T(8,128)}, u32[]{:S(2)}) copy-start(f32[128,128]{1,0:T(8,128)} %fusion.57) | copy-start | bytes 196612
  131.6 3.8 %copy-start.8 = (f32[128,64]{0,1:T(8,128)S(1)}, f32[128,64]{0,1:T(8,128)}, u32[]{:S(2)}) copy-start(f32[128,64]{0,1:T(8,128)} %copy.81) | copy-start | bytes 98308
  131.6 3.8 %copy-start.11 = (f32[1,128,64]{1,2,0:T(8,128)S(1)}, f32[1,128,64]{1,2,0:T(8,128)}, u32[]{:S(2)}) copy-start(f32[1,128,64]{1,2,0:T(8,128)} %copy.78) | copy-start | bytes 98308
  131.7 3.8 %copy-start.15 = (pred[128,128]{1,0:T(8,128)(4,1)S(1)}, pred[128,128]{1,0:T(8,128)(4,1)}, u32[]{:S(2)}) copy-start(pred[128,128]{1,0:T(8,128)(4,1)} %copy.79) | copy-start | bytes 49156
  135.5 8.3 %copy-start.10 = (f32[128,64]{0,1:T(8,128)S(1)}, f32[128,64]{0,1:T(8,128)}, u32[]{:S(2)}) copy-start(f32[128,64]{0,1:T(8,128)} %get-tuple-element.44) | copy-start | bytes 98308
  151.4 8.2 %copy-start.4 = (bf16[1,128,4096]{1,2,0:T(8,128)(2,1)S(1)}, bf16[1,128,4096]{1,2,0:T(8,128)(2,1)}, u32[]{:S(2)}) copy-start(bf16[1,128,4096]{1,2,0:T(8,128)(2,1)} %copy.80) | copy-start | bytes 3145732
  154.4 5.2 %copy-start.2 = (f32[1,128,4096]{1,2,0:T(8,128)S(1)}, f32[1,128,4096]{1,2,0:T(8,128)}, u32[]{:S(2)}) copy-start(f32[1,128,4096]{1,2,0:T(8,128)} %convert_element_type.57) | copy-start | bytes 6291460
  154.4 5.2 %copy-start.9 = (f32[128,64]{0,1:T(8,128)S(1)}, f32[128,64]{0,1:T(8,128)}, u32[]{:S(2)}) copy-start(f32[128,64]{0,1:T(8,128)} %copy.81) | copy-start | bytes 98308
  154.4 5.2 %copy-start.12 = (f32[1,128,64]{1,2,0:T(8,128)S(1)}, f32[1,128,64]{1,2,0:T(8,128)}, u32[]{:S(2)}) copy-start(f32[1,128,64]{1,2,0:T(8,128)} %copy.78) | copy-start | bytes 98308
  154.4 5.2 %copy-start.13 = (f32[128,128]{0,1:T(8,128)S(1)}, f32[128,128]{0,1:T(8,128)}, u32[]{:S(2)}) copy-start(f32[128,128]{0,1:T(8,128)} %copy.93) | copy-start | bytes 196612
  169.4 3.0 copy-start.14
  169.4 3.1 copy-start.5
  169.4 3.1 copy-start.7
  169.4 3.1 copy-start.18
  169.4 3.1 copy-start.19
  169.4 3.1 copy-start.21
  169.4 4.3 %copy-start.16 = (f32[1,64]{1,0:T(1,128)S(1)}, f32[1,64]{1,0:T(1,128)}, u32[]{:S(2)}) copy-start(f32[1,64]{1,0:T(1,128)} %param.10) | copy-start | bytes 772
  169.4 4.3 %copy-start.17 = (f32[64]{0:T(128)S(1)}, f32[64]{0:T(128)}, u32[]{:S(2)}) copy-start(f32[64]{0:T(128)} %exponential_bitcast_fusion) | copy-start | bytes 772
  179.9 196.4 %reduce-scatter.8.cloned.1.call-start = ((), (), s32[]{:S(2)}) async-start(), calls=%async_computation.4 | async-start | bytes 11796480 | tf_op jit(solution)/shard_map/reduce_scatter | solution.py:89
  196.9 0.7 copy-start.20
Sparse Core Ops, SparseCore 0:
  10.2 88.9 all-gather.2
  104.6 5.9 reduce-scatter.5
  180.0 8.4 reduce-scatter.9
  197.1 179.2 reduce-scatter.7
where the time goes:
time: 384 us; the launch traced here: 383 us
  waiting for transfers between devices  270 us (70%)
  matrix products  51 us (13%)
  local copies, waits for them, and re-layouts  22.5 us (6%)
  other arithmetic  18.3 us (5%)
  between operations  14.2 us (4%)
  blocking collectives  4.16 us (1%)
    reduce_scatter x1, waiting for transfers between devices, per_device(): lax.psum_scatter(lax.dot_general(proj_grad, inputs, (((0,), (0,)), ((), (...  172 us
    all_gather x1, waiting for transfers between devices, per_device(): weight_full = lax.all_gather(weight_local, 'fsdp', axis=1, tiled=True)  88.2 us
    dot_general x2, matrix products, state_space(): within = jnp.einsum('kijh,kjhp->kihp', mixing, scaled, precision=highest)  14.2 us
    dot_general x2, matrix products, state_space(): jnp.einsum('kjn,kjhp->khnp', b_blocks, scaled * to_end[..., None], precis...  9.78 us
    reduce_scatter x2, waiting for transfers between devices, head_share(): return lax.psum_scatter(partial_sums, 'tp', scatter_dimension=0, tiled=True)  8.57 us
  transfers between devices with their start and end apart: 5, of which 3 were waited for; matrix products, arithmetic and copies ran while one was open for 5% of the time, Pallas kernels for 0%

commit v1 on v0

--- a/solution.py
+++ b/solution.py
@@ -1,6 +1,10 @@
+import functools
+
 import jax
 import jax.numpy as jnp
 from jax import lax
+from jax.experimental import pallas as pl
+from jax.experimental.pallas import tpu as pltpu
 from jax.sharding import PartitionSpec as P
 
 HEAD_DIM = 64
@@ -98,6 +102,427 @@
     return (grad_inputs[None], section_wgrad[None])
 
 
+MESH = pl.DeviceIdType.MESH
+F32 = jnp.float32
+BF16 = jnp.bfloat16
+GROUP = 8
+
+
+def fits(mesh):
+    return mesh.shape["tp"] == 2 and mesh.shape["fsdp"] == 8
+
+
+def times(left, right, over, precision=None):
+    return lax.dot_general(
+        left, right, ((over[:1], over[1:]), ((), ())),
+        precision=precision, preferred_element_type=F32,
+    )
+
+
+def fused_kernel(
+    line, pairs,
+    x_ref, ret_ref, w_ref, rate_ref, bias_ref, gain_ref,
+    out_ref, wg_ref,
+    arrived, x_other, w_all, proj, proj_tp, proj_theirs, projs,
+    dt_s, cum_s, ddt_s, rs_s, ds_s, ds_in, raw_out, raw_in, gx,
+    pg_x, pg_in, up_out, dn_out, up_in, dn_in,
+    local_sem, ret_sem, x_sem, wz_recv, wz_up, wz_dn, wx_send, wx_recv,
+    pj_send, pj_recv, tp_sem, ds_sem, raw_sem, pg_sem, up_send, up_recv, dn_send, dn_recv,
+):
+    exact = lax.Precision.HIGHEST
+    pp_count = lax.axis_size("pp")
+    pp, f, tp = lax.axis_index("pp"), lax.axis_index("fsdp"), lax.axis_index("tp")
+    z, x = f // 2, f % 2
+    width, inner = w_ref.shape
+    rows = x_ref.shape[0]
+    heads = rate_ref.shape[0]
+    last = line - 1
+    before = {"pp": lax.rem(pp + pp_count - 1, pp_count)}
+    after = {"pp": lax.rem(pp + 1, pp_count)}
+    side = {"fsdp": f + 1 - 2 * x}
+    core = {"tp": 1 - tp}
+    above, below = {"fsdp": f + 2}, {"fsdp": f - 2}
+
+    def remote(src, dst, send, recv, where):
+        return pltpu.make_async_remote_copy(
+            src_ref=src, dst_ref=dst, send_sem=send, recv_sem=recv,
+            device_id=where, device_id_type=MESH,
+        )
+
+    barrier = pltpu.get_barrier_semaphore()
+    greeted = [side, core, before] + ([after] if pairs > 2 else [])
+    for where in greeted:
+        pl.semaphore_signal(barrier, inc=1, device_id=where, device_id_type=MESH)
+
+    @pl.when(z > 0)
+    def _():
+        pl.semaphore_signal(barrier, inc=1, device_id=below, device_id_type=MESH)
+
+    @pl.when(z < last)
+    def _():
+        pl.semaphore_signal(barrier, inc=1, device_id=above, device_id_type=MESH)
+
+    ends = jnp.where(z > 0, 1, 0) + jnp.where(z < last, 1, 0)
+    pl.semaphore_wait(barrier, len(greeted) + ends)
+
+    own_w = pltpu.make_async_copy(w_ref, w_all.at[z, x], local_sem)
+    own_w.start()
+
+    def w_up(block, s):
+        src = w_ref if s == 0 else w_all.at[block, x]
+        return remote(src, w_all.at[block, x], wz_up.at[s], wz_recv.at[block], above)
+
+    def w_dn(block, s):
+        src = w_ref if s == 0 else w_all.at[block, x]
+        return remote(src, w_all.at[block, x], wz_dn.at[s], wz_recv.at[block], below)
+
+    def w_side(block):
+        return remote(
+            w_all.at[block, x], w_all.at[block, x], wx_send.at[block], wx_recv.at[block], side
+        )
+
+    @pl.when(z < last)
+    def _():
+        w_up(z, 0).start()
+
+    @pl.when(z > 0)
+    def _():
+        w_dn(z, 0).start()
+
+    x_copy = remote(x_ref, x_other, x_sem.at[0], x_sem.at[1], side)
+    x_copy.start()
+    ret_copy = remote(ret_ref, arrived, ret_sem.at[0], ret_sem.at[1], before)
+    ret_copy.start()
+
+    def pj_copy(block):
+        return remote(
+            proj_theirs.at[block], proj.at[block, x], pj_send.at[block], pj_recv.at[block], side
+        )
+
+    def project(block):
+        weight = w_all[block, x]
+        proj_theirs[block] = times(weight, x_other[...], (1, 1))
+        pj_copy(block).start()
+        proj[block, x] = times(weight, x_ref[...], (1, 1))
+
+    own_w.wait()
+    x_copy.wait_recv()
+    w_side(z).start()
+    project(z)
+    for s in range(1, line):
+        low, high = z - s, z + s
+
+        @pl.when(low >= 0)
+        def _():
+            w_dn(low, s - 1).wait_recv()
+            if s < line - 1:
+                @pl.when(z < last)
+                def _():
+                    w_up(low, s).start()
+            project(low)
+
+        @pl.when(high <= last)
+        def _():
+            w_up(high, s - 1).wait_recv()
+            if s < line - 1:
+                @pl.when(z > 0)
+                def _():
+                    w_dn(high, s).start()
+            project(high)
+
+    for block in range(line):
+        remote(
+            proj_theirs.at[block], proj.at[block, 1 - x], pj_send.at[block], pj_recv.at[block], side
+        ).wait_recv()
+    tp_copy = remote(proj, proj_tp, tp_sem.at[0], tp_sem.at[1], core)
+    tp_copy.start()
+    tp_copy.wait_recv()
+    projs[...] = (proj[...] + proj_tp[...]).reshape(projs.shape)
+
+    for block in range(line):
+        @pl.when(block != z)
+        def _():
+            w_side(block).start()
+
+    row_at = lax.broadcasted_iota(jnp.int32, (rows, rows), 0)
+    column_at = lax.broadcasted_iota(jnp.int32, (rows, rows), 1)
+    causal = row_at >= column_at
+    lower = causal.astype(F32)
+    upper = (row_at <= column_at).astype(F32)
+    b_t, c_t = projs[:STATE], projs[STATE : 2 * STATE]
+    start = pl.multiple_of(2 * STATE + tp * heads, 8)
+    raw = projs[pl.ds(start, heads)] + bias_ref[...]
+    step = jnp.maximum(raw, 0.0) + jnp.log1p(jnp.exp(-jnp.abs(raw)))
+    decay = -jnp.exp(rate_ref[...])
+    groups = heads // GROUP
+    cum_s[...] = times(step * decay, upper, (1, 0), exact).reshape(groups, GROUP, rows)
+    dt_s[...] = step.reshape(groups, GROUP, rows)
+    scores = times(c_t, b_t, (0, 0), exact)
+    ds_s[...] = jnp.zeros_like(ds_s)
+    pair_lanes = 2 * HEAD_DIM
+    lane = lax.broadcasted_iota(jnp.int32, (rows, pair_lanes), 1)
+    ret_copy.wait_recv()
+
+    def group_step(g, carry):
+        cum_rows = cum_s[g]
+        cum_columns = cum_rows.T
+        dt_rows = dt_s[g]
+        ddt_rows, rs_columns = [], []
+        for p in range(GROUP // 2):
+            at = pl.multiple_of(g * (GROUP * HEAD_DIM) + p * pair_lanes, pair_lanes)
+            g_pair = arrived[:, pl.ds(at, pair_lanes)]
+            x_pair = x_ref[:, pl.ds(at, pair_lanes)]
+            g_wide = g_pair.astype(F32)
+            g_both = jnp.concatenate(
+                [
+                    jnp.where(lane < HEAD_DIM, g_wide, 0.0).astype(BF16),
+                    jnp.where(lane < HEAD_DIM, 0.0, g_wide).astype(BF16),
+                ],
+                axis=0,
+            )
+            products = times(g_both, x_pair, (1, 1))
+            mixed, ds_part = [], None
+            for e in range(2):
+                h = 2 * p + e
+                dt_row = dt_rows[h : h + 1]
+                gap = cum_columns[:, h : h + 1] - cum_rows[h : h + 1]
+                mask = jnp.exp(jnp.where(causal, gap, -1e30))
+                product = products[e * rows : (e + 1) * rows]
+                with_scores = mask * scores
+                total = with_scores * product
+                ddt_rows.append(jnp.sum(total, axis=0, keepdims=True))
+                rs_columns.append(jnp.sum(total * dt_row, axis=1, keepdims=True))
+                part = mask * product * dt_row
+                ds_part = part if ds_part is None else ds_part + part
+                mixed.append((with_scores * dt_row).astype(BF16))
+            ds_s[...] += ds_part
+            dx = times(jnp.concatenate(mixed, axis=0), g_both, (0, 0))
+            gx[:, pl.ds(at, pair_lanes)] = dx + (1.0 + gain_ref[:, pl.ds(at, pair_lanes)]) * g_wide
+        ddt_s[g] = jnp.concatenate(ddt_rows, axis=0)
+        rs_s[g] = jnp.concatenate(rs_columns, axis=1).T
+        return carry
+
+    lax.fori_loop(0, groups, group_step, 0)
+    ds_copy = remote(ds_s, ds_in, ds_sem.at[0], ds_sem.at[1], core)
+    ds_copy.start()
+    ddt = ddt_s[...].reshape(heads, rows)
+    d_cum = rs_s[...].reshape(heads, rows) - step * ddt
+    d_decay = times(d_cum, lower, (1, 0), exact)
+    raw_out[...] = ((ddt + d_decay * decay) * (1.0 / (1.0 + jnp.exp(-raw)))).astype(BF16)
+    raw_copy = remote(raw_out, raw_in, raw_sem.at[0], raw_sem.at[1], core)
+    raw_copy.start()
+    ds_copy.wait_recv()
+    ds_total = ds_s[...] + ds_in[...]
+    grad_b = times(c_t, ds_total, (1, 0), exact).astype(BF16)
+    grad_c = times(b_t, ds_total, (1, 1), exact).astype(BF16)
+    raw_copy.wait_recv()
+    mine, other = raw_out[...].astype(F32), raw_in[...].astype(F32)
+    first = jnp.where(tp == 0, mine, other).astype(BF16)
+    second = jnp.where(tp == 0, other, mine).astype(BF16)
+    proj_grad = jnp.concatenate([grad_b, grad_c, first, second], axis=0)
+    blocks = proj_grad.reshape(line, 2, width, rows)
+    pg_x[0] = blocks[:, 0]
+    pg_x[1] = blocks[:, 1]
+    pg_copy = remote(pg_x.at[1 - x], pg_in, pg_sem.at[0], pg_sem.at[1], side)
+    pg_copy.start()
+    pg_copy.wait_recv()
+
+    tile = 512
+
+    def partial(block, at):
+        return times(pg_x[x, block], x_ref[:, pl.ds(at, tile)], (1, 0)) + times(
+            pg_in[block], x_other[:, pl.ds(at, tile)], (1, 0)
+        )
+
+    def sums(block, sink, *more):
+        def body(i, carry):
+            at = pl.multiple_of(i * tile, tile)
+            value = partial(block, at)
+            for ref in more:
+                value = value + ref[block, :, pl.ds(at, tile)].astype(F32)
+            sink(at, value)
+            return carry
+
+        lax.fori_loop(0, inner // tile, body, 0)
+
+    def up_copy(block):
+        return remote(up_out.at[block], up_in.at[block], up_send.at[block], up_recv.at[block], above)
+
+    def dn_copy(block):
+        return remote(dn_out.at[block], dn_in.at[block], dn_send.at[block], dn_recv.at[block], below)
+
+    def into(ref, block):
+        def sink(at, value):
+            ref[block, :, pl.ds(at, tile)] = value.astype(BF16)
+
+        return sink
+
+    @pl.when(z == 0)
+    def _():
+        for block in range(last, 0, -1):
+            sums(block, into(up_out, block))
+            up_copy(block).start()
+
+    @pl.when(z == last)
+    def _():
+        for block in range(last):
+            sums(block, into(dn_out, block))
+            dn_copy(block).start()
+
+    for block in range(line):
+        remote(
+            w_all.at[block, x], w_all.at[block, 1 - x], wx_send.at[block], wx_recv.at[block], side
+        ).wait_recv()
+
+    turned = proj_grad.astype(F32).T.astype(BF16)
+
+    def back(i, carry):
+        at = pl.multiple_of(i * tile, tile)
+        weight = w_all[:, :, :, pl.ds(at, tile)].reshape(line * 2 * width, tile)
+        out_ref[:, pl.ds(at, tile)] = (
+            gx[:, pl.ds(at, tile)] + times(turned, weight, (1, 0))
+        ).astype(BF16)
+        return carry
+
+    @pl.when(jnp.logical_or(z == 0, z == last))
+    def _():
+        lax.fori_loop(0, inner // tile, back, 0)
+
+    for k in range(last):
+        up_block, dn_block = last - k, k
+
+        @pl.when(jnp.logical_and(z > 0, z < up_block))
+        def _():
+            dn = remote(
+                up_out.at[up_block], up_in.at[up_block], up_send.at[up_block],
+                up_recv.at[up_block], below,
+            )
+            dn.wait_recv()
+            sums(up_block, into(up_out, up_block), up_in)
+            up_copy(up_block).start()
+
+        @pl.when(jnp.logical_and(z < last, z > dn_block))
+        def _():
+            up = remote(
+                dn_out.at[dn_block], dn_in.at[dn_block], dn_send.at[dn_block],
+                dn_recv.at[dn_block], above,
+            )
+            up.wait_recv()
+            sums(dn_block, into(dn_out, dn_block), dn_in)
+            dn_copy(dn_block).start()
+
+    @pl.when(jnp.logical_and(z > 0, z < last))
+    def _():
+        lax.fori_loop(0, inner // tile, back, 0)
+
+    def final(at, value):
+        wg_ref[:, pl.ds(at, tile)] = value
+
+    def from_below():
+        remote(up_out.at[z], up_in.at[z], up_send.at[z], up_recv.at[z], below).wait_recv()
+
+    def from_above():
+        remote(dn_out.at[z], dn_in.at[z], dn_send.at[z], dn_recv.at[z], above).wait_recv()
+
+    @pl.when(z == 0)
+    def _():
+        from_above()
+        sums(z, final, dn_in)
+
+    @pl.when(z == last)
+    def _():
+        from_below()
+        sums(z, final, up_in)
+
+    @pl.when(jnp.logical_and(z > 0, z < last))
+    def _():
+        from_below()
+        from_above()
+        sums(z, final, up_in, dn_in)
+
+    for copy in (x_copy, ret_copy, tp_copy, ds_copy, raw_copy, pg_copy):
+        copy.wait_send()
+    for block in range(line):
+        pj_copy(block).wait_send()
+        w_side(block).wait_send()
+
+        @pl.when(block > z)
+        def _():
+            up_copy(block).wait_send()
+
+        @pl.when(block < z)
+        def _():
+            dn_copy(block).wait_send()
+
+    for s in range(line - 1):
+        @pl.when(jnp.logical_and(z < last, z - s >= 0))
+        def _():
+            w_up(z - s, s).wait_send()
+
+        @pl.when(jnp.logical_and(z > 0, z + s <= last))
+        def _():
+            w_dn(z + s, s).wait_send()
+
+
+def fused_device(saved_inputs, returned, proj_weight, log_rate, step_bias, skip_gain):
+    inputs = saved_inputs[0]
+    rows, inner = inputs.shape
+    heads = log_rate.shape[1]
+    width = proj_weight.shape[2]
+    line = lax.axis_size("fsdp") // 2
+    columns = line * 2 * width
+    groups = heads // GROUP
+    vmem = pl.BlockSpec(memory_space=pltpu.VMEM)
+    dma = pltpu.SemaphoreType.DMA
+    grad_out, share = pl.pallas_call(
+        functools.partial(fused_kernel, line, lax.axis_size("pp")),
+        out_shape=(
+            jax.ShapeDtypeStruct((rows, inner), BF16),
+            jax.ShapeDtypeStruct((width, inner), F32),
+        ),
+        in_specs=[vmem] * 6,
+        out_specs=(vmem, vmem),
+        scratch_shapes=[
+            pltpu.VMEM((rows, inner), BF16),
+            pltpu.VMEM((rows, inner), BF16),
+            pltpu.VMEM((line, 2, width, inner), BF16),
+            pltpu.VMEM((line, 2, width, rows), F32),
+            pltpu.VMEM((line, 2, width, rows), F32),
+            pltpu.VMEM((line, width, rows), F32),
+            pltpu.VMEM((columns, rows), F32),
+            pltpu.VMEM((groups, GROUP, rows), F32),
+            pltpu.VMEM((groups, GROUP, rows), F32),
+            pltpu.VMEM((groups, GROUP, rows), F32),
+            pltpu.VMEM((groups, GROUP, rows), F32),
+            pltpu.VMEM((rows, rows), F32),
+            pltpu.VMEM((rows, rows), F32),
+            pltpu.VMEM((heads, rows), BF16),
+            pltpu.VMEM((heads, rows), BF16),
+            pltpu.VMEM((rows, inner), F32),
+            pltpu.VMEM((2, line, width, rows), BF16),
+            pltpu.VMEM((line, width, rows), BF16),
+            pltpu.VMEM((line, width, inner), BF16),
+            pltpu.VMEM((line, width, inner), BF16),
+            pltpu.VMEM((line, width, inner), BF16),
+            pltpu.VMEM((line, width, inner), BF16),
+            dma, dma((2,)), dma((2,)), dma((line,)), dma((line,)), dma((line,)),
+            dma((line,)), dma((line,)), dma((line,)), dma((line,)), dma((2,)), dma((2,)),
+            dma((2,)), dma((2,)), dma((line,)), dma((line,)), dma((line,)), dma((line,)),
+        ],
+        compiler_params=pltpu.CompilerParams(
+            collective_id=0, has_side_effects=True, vmem_limit_bytes=48 * 1024 * 1024
+        ),
+    )(
+        inputs,
+        returned[0],
+        proj_weight[0].T,
+        log_rate[0][:, None],
+        step_bias[0][:, None],
+        jnp.repeat(skip_gain[0], HEAD_DIM)[None, :],
+    )
+    return (grad_out[None], share.T[None])
+
+
 def solution(mesh):
     placed = (
         P("pp", "fsdp", "tp"),
@@ -108,7 +533,7 @@
         P("pp", "tp"),
     )
     return jax.shard_map(
-        per_device,
+        fused_device if fits(mesh) else per_device,
         mesh=mesh,
         in_specs=placed,
         out_specs=(P("pp", "fsdp", "tp"), P("pp", "tp", "fsdp")),

time: 384 us -> 192 us (0.50)
  waiting for transfers between devices: 270 us -> 0 us
  Pallas kernels: 0 us -> 183 us
  matrix products: 51 us -> 0 us
  other arithmetic: 18.3 us -> 0 us
  local copies, waits for them, and re-layouts: 22.5 us -> 7.86 us
  between operations: 14.2 us -> 0.66 us
  blocking collectives: 4.16 us -> 0 us
    pallas_call x0 -> x1, Pallas kernels: none -> 183 us  [fused_device(): pl.pallas_call(functools.partial(fused_kernel, line, lax.axis_size('pp'))...]
    reduce_scatter x3 -> x0, waiting for transfers between devices: 181 us -> none  [the longest x1 172 us: per_device(): lax.psum_scatter(lax.dot_general(proj_grad, inputs, (((0,), (0,)), ((), (...]
    all_gather x1 -> x0, waiting for transfers between devices: 88.2 us -> none  [per_device(): weight_full = lax.all_gather(weight_local, 'fsdp', axis=1, tiled=True)]
    dot_general x11 -> x0, matrix products: 46.2 us -> none  [the longest x2 14.2 us: state_space(): within = jnp.einsum('kijh,kjhp->kihp', mixing, scaled, precision=highest)]
    mul x7 -> x0, local copies, waits for them, and re-layouts: 8.21 us -> none  [the longest x3 7.4 us: state_space(): jnp.einsum('kin,khnp->kihp', c_blocks, entering, precision=highest)]
    mul x4 -> x0, other arithmetic: 6.73 us -> none  [the longest x1 3.14 us: state_space(): jnp.einsum('kin,khnp->kihp', c_blocks, entering, precision=highest)]
    unnamed x1 -> x0, matrix products: 4.8 us -> none
    all_gather x2 -> x0, blocking collectives: 4.16 us -> none  [the longest x1 2.24 us: per_device(): lax.all_gather(head_share(partial_proj), 'tp', axis=0, tiled=True)]
  transfers between devices with their start and end apart: 5 -> 0, of which waited for: 3 -> 0; matrix products, arithmetic and copies ran while one was open for 5% -> 0% of each run, Pallas kernels for 0% -> 0%
where the time goes in v1:
time: 192 us; the launch traced here: 191 us
  Pallas kernels  183 us (95%)
  local copies, waits for them, and re-layouts  7.86 us (4%)
    pallas_call x1, Pallas kernels, fused_device(): pl.pallas_call(functools.partial(fused_kernel, line, lax.axis_size('pp'))...  183 us
    unnamed x8, local copies, waits for them, and re-layouts  5.56 us

profile of v1, /device:TPU:0, one launch (start us, length us, event | category | flops | bytes accessed | tf_op | source)
XLA Modules:
  0.0 191.4 jit_solution(7458219972527589547)
XLA Ops:
  0.6 0.7 copy.8.rate_ref
  1.4 0.7 copy.9.bias_ref
  2.1 0.7 broadcast_in_dim.9
  2.8 0.1 broadcast_in_dim_reshape.3.gain_ref
  2.9 0.0 copy-start
  3.0 1.2 copy-done
  4.2 0.0 copy-start.1
  4.2 1.2 copy-done.1
  5.4 0.0 copy-start.2
  5.4 1.1 copy-done.2
  6.5 182.9 %shard_map.77 = (bf16[128,4096]{1,0:T(8,128)(2,1)S(1)}, f32[80,4096]{1,0:T(8,128)S(1)}) custom-call(bf16[128,4096]{1,0:T(8,128)(2,1)S(1)} %bitcast.14, bf16[128,4096]{1,0:T(8,128)(2,1)S(1)} %bitcast.15, bf16[80,4096]{1,0:T(8,128)(2,1)S(1)} %bitcast.16, f32[64,1]{1,0:T(8,128)S(1)} %copy.8.rate_ref, f32[64,1]{1,0:T(8,128)S(1)} %copy.9.bias_ref, ...), custom_call_target="tpu_custom_call" | custom-call | tf_op jit(solution)/shard_map/pallas_call | solution.py:477
  189.4 1.0 copy.12
  190.3 1.1 copy.13
Async XLA Ops:
  2.9 1.2 copy-start
  4.2 1.2 copy-start.1
  5.4 1.1 copy-start.2

commit v2 on v1

--- a/solution.py
+++ b/solution.py
@@ -121,12 +121,13 @@
 
 def fused_kernel(
     line, pairs,
-    x_ref, ret_ref, w_ref, rate_ref, bias_ref, gain_ref,
+    x_hbm, ret_ref, w_ref, rate_ref, bias_ref, gain_ref,
     out_ref, wg_ref,
+    x_ref, gain_s, xa, pg_z, pg_a, parts, side_out, side_in,
     arrived, x_other, w_all, proj, proj_tp, proj_theirs, projs,
     dt_s, cum_s, ddt_s, rs_s, ds_s, ds_in, raw_out, raw_in, gx,
     pg_x, pg_in, up_out, dn_out, up_in, dn_in,
-    local_sem, ret_sem, x_sem, wz_recv, wz_up, wz_dn, wx_send, wx_recv,
+    local_sem, local_x, local_a, xa_recv, xa_up, xa_dn, pa_send, pa_recv, side_sem, ret_sem, x_sem, wz_recv, wz_up, wz_dn, wx_send, wx_recv,
     pj_send, pj_recv, tp_sem, ds_sem, raw_sem, pg_sem, up_send, up_recv, dn_send, dn_recv,
 ):
     exact = lax.Precision.HIGHEST
@@ -135,7 +136,8 @@
     z, x = f // 2, f % 2
     width, inner = w_ref.shape
     rows = x_ref.shape[0]
-    heads = rate_ref.shape[0]
+    heads = rate_ref.shape[1]
+    wide = xa.shape[2]
     last = line - 1
     before = {"pp": lax.rem(pp + pp_count - 1, pp_count)}
     after = {"pp": lax.rem(pp + 1, pp_count)}
@@ -154,19 +156,14 @@
     for where in greeted:
         pl.semaphore_signal(barrier, inc=1, device_id=where, device_id_type=MESH)
 
-    @pl.when(z > 0)
-    def _():
-        pl.semaphore_signal(barrier, inc=1, device_id=below, device_id_type=MESH)
-
-    @pl.when(z < last)
-    def _():
-        pl.semaphore_signal(barrier, inc=1, device_id=above, device_id_type=MESH)
-
-    ends = jnp.where(z > 0, 1, 0) + jnp.where(z < last, 1, 0)
-    pl.semaphore_wait(barrier, len(greeted) + ends)
+    for k in range(1, line):
+        along = {"fsdp": 2 * lax.rem(z + k, line) + x}
+        pl.semaphore_signal(barrier, inc=1, device_id=along, device_id_type=MESH)
+    pl.semaphore_wait(barrier, len(greeted) + line - 1)
 
     own_w = pltpu.make_async_copy(w_ref, w_all.at[z, x], local_sem)
-    own_w.start()
+    own_x = pltpu.make_async_copy(x_hbm, x_ref, local_x)
+    own_a = pltpu.make_async_copy(x_hbm.at[:, pl.ds(0, wide)], xa.at[z], local_a)
 
     def w_up(block, s):
         src = w_ref if s == 0 else w_all.at[block, x]
@@ -189,10 +186,13 @@
     def _():
         w_dn(z, 0).start()
 
-    x_copy = remote(x_ref, x_other, x_sem.at[0], x_sem.at[1], side)
+    x_copy = remote(x_hbm, x_other, x_sem.at[0], x_sem.at[1], side)
     x_copy.start()
     ret_copy = remote(ret_ref, arrived, ret_sem.at[0], ret_sem.at[1], before)
     ret_copy.start()
+    own_w.start()
+    own_x.start()
+    own_a.start()
 
     def pj_copy(block):
         return remote(
@@ -206,6 +206,8 @@
         proj[block, x] = times(weight, x_ref[...], (1, 1))
 
     own_w.wait()
+    own_x.wait()
+    own_a.wait()
     x_copy.wait_recv()
     w_side(z).start()
     project(z)
@@ -230,6 +232,34 @@
                     w_dn(high, s).start()
             project(high)
 
+    def xa_up_copy(block, s):
+        return remote(xa.at[block], xa.at[block], xa_up.at[s], xa_recv.at[block], above)
+
+    def xa_dn_copy(block, s):
+        return remote(xa.at[block], xa.at[block], xa_dn.at[s], xa_recv.at[block], below)
+
+    def xa_pass(s):
+        low, high = z - s, z + s
+
+        @pl.when(low >= 0)
+        def _():
+            if s > 0:
+                xa_dn_copy(low, s - 1).wait_recv()
+            if s < line - 1:
+                @pl.when(z < last)
+                def _():
+                    xa_up_copy(low, s).start()
+
+        @pl.when(high <= last)
+        def _():
+            if s > 0:
+                xa_up_copy(high, s - 1).wait_recv()
+            if s < line - 1:
+                @pl.when(z > 0)
+                def _():
+                    xa_dn_copy(high, s).start()
+
+    xa_pass(0)
     for block in range(line):
         remote(
             proj_theirs.at[block], proj.at[block, 1 - x], pj_send.at[block], pj_recv.at[block], side
@@ -239,10 +269,8 @@
     tp_copy.wait_recv()
     projs[...] = (proj[...] + proj_tp[...]).reshape(projs.shape)
 
-    for block in range(line):
-        @pl.when(block != z)
-        def _():
-            w_side(block).start()
+    for k in range(1, line - 1):
+        w_side(lax.rem(z + k, line)).start()
 
     row_at = lax.broadcasted_iota(jnp.int32, (rows, rows), 0)
     column_at = lax.broadcasted_iota(jnp.int32, (rows, rows), 1)
@@ -251,10 +279,11 @@
     upper = (row_at <= column_at).astype(F32)
     b_t, c_t = projs[:STATE], projs[STATE : 2 * STATE]
     start = pl.multiple_of(2 * STATE + tp * heads, 8)
-    raw = projs[pl.ds(start, heads)] + bias_ref[...]
+    raw = projs[pl.ds(start, heads)] + jnp.broadcast_to(bias_ref[...], (rows, heads)).T
     step = jnp.maximum(raw, 0.0) + jnp.log1p(jnp.exp(-jnp.abs(raw)))
-    decay = -jnp.exp(rate_ref[...])
+    decay = -jnp.exp(jnp.broadcast_to(rate_ref[...], (rows, heads)).T)
     groups = heads // GROUP
+    gain_s[...] = jnp.broadcast_to(gain_ref[...], (rows, heads)).T.reshape(groups, GROUP, rows)
     cum_s[...] = times(step * decay, upper, (1, 0), exact).reshape(groups, GROUP, rows)
     dt_s[...] = step.reshape(groups, GROUP, rows)
     scores = times(c_t, b_t, (0, 0), exact)
@@ -267,6 +296,12 @@
         cum_rows = cum_s[g]
         cum_columns = cum_rows.T
         dt_rows = dt_s[g]
+        gain_rows = gain_s[g]
+
+        @pl.when(g == groups // 2)
+        def _():
+            xa_pass(1)
+
         ddt_rows, rs_columns = [], []
         for p in range(GROUP // 2):
             at = pl.multiple_of(g * (GROUP * HEAD_DIM) + p * pair_lanes, pair_lanes)
@@ -297,7 +332,10 @@
                 mixed.append((with_scores * dt_row).astype(BF16))
             ds_s[...] += ds_part
             dx = times(jnp.concatenate(mixed, axis=0), g_both, (0, 0))
-            gx[:, pl.ds(at, pair_lanes)] = dx + (1.0 + gain_ref[:, pl.ds(at, pair_lanes)]) * g_wide
+            gain = jnp.where(
+                lane[:1] < HEAD_DIM, gain_rows[2 * p : 2 * p + 1], gain_rows[2 * p + 1 : 2 * p + 2]
+            )
+            gx[:, pl.ds(at, pair_lanes)] = dx + (1.0 + gain) * g_wide
         ddt_s[g] = jnp.concatenate(ddt_rows, axis=0)
         rs_s[g] = jnp.concatenate(rs_columns, axis=1).T
         return carry
@@ -305,6 +343,7 @@
     lax.fori_loop(0, groups, group_step, 0)
     ds_copy = remote(ds_s, ds_in, ds_sem.at[0], ds_sem.at[1], core)
     ds_copy.start()
+    xa_pass(2)
     ddt = ddt_s[...].reshape(heads, rows)
     d_cum = rs_s[...].reshape(heads, rows) - step * ddt
     d_decay = times(d_cum, lower, (1, 0), exact)
@@ -320,61 +359,112 @@
     first = jnp.where(tp == 0, mine, other).astype(BF16)
     second = jnp.where(tp == 0, other, mine).astype(BF16)
     proj_grad = jnp.concatenate([grad_b, grad_c, first, second], axis=0)
-    blocks = proj_grad.reshape(line, 2, width, rows)
-    pg_x[0] = blocks[:, 0]
-    pg_x[1] = blocks[:, 1]
+    pg_z[...] = proj_grad.reshape(line, 2, width, rows)
+    pg_x[...] = jnp.stack([pg_z[:, 0], pg_z[:, 1]], axis=0)
     pg_copy = remote(pg_x.at[1 - x], pg_in, pg_sem.at[0], pg_sem.at[1], side)
     pg_copy.start()
+
+    def pa_copy(k):
+        to = lax.rem(z + k, line)
+        return remote(
+            pg_z.at[to], pg_a.at[z], pa_send.at[k], pa_recv.at[k], {"fsdp": 2 * to + x}
+        )
+
+    for k in range(1, line):
+        pa_copy(k).start()
+    turned = proj_grad.astype(F32).T.astype(BF16)
+    pg_a[z] = pg_z[z]
     pg_copy.wait_recv()
+    w_side(lax.rem(z + line - 1, line)).start()
 
     tile = 512
-
-    def partial(block, at):
-        return times(pg_x[x, block], x_ref[:, pl.ds(at, tile)], (1, 0)) + times(
-            pg_in[block], x_other[:, pl.ds(at, tile)], (1, 0)
-        )
-
-    def sums(block, sink, *more):
+    chunk = parts.shape[3]
+    chunks = parts.shape[0]
+    both = jnp.concatenate(
+        [pg_x[x].reshape(line * width, rows), pg_in[...].reshape(line * width, rows)], axis=1
+    )
+
+    def part(c):
         def body(i, carry):
             at = pl.multiple_of(i * tile, tile)
-            value = partial(block, at)
-            for ref in more:
-                value = value + ref[block, :, pl.ds(at, tile)].astype(F32)
-            sink(at, value)
+            here = pl.multiple_of(wide + c * chunk + i * tile, tile)
+            tokens = jnp.concatenate(
+                [x_ref[:, pl.ds(here, tile)], x_other[:, pl.ds(here, tile)]], axis=0
+            )
+            value = times(both, tokens, (1, 0))
+            parts[c, :, :, pl.ds(at, tile)] = value.reshape(line, width, tile)
             return carry
 
-        lax.fori_loop(0, inner // tile, body, 0)
-
-    def up_copy(block):
-        return remote(up_out.at[block], up_in.at[block], up_send.at[block], up_recv.at[block], above)
-
-    def dn_copy(block):
-        return remote(dn_out.at[block], dn_in.at[block], dn_send.at[block], dn_recv.at[block], below)
-
-    def into(ref, block):
-        def sink(at, value):
-            ref[block, :, pl.ds(at, tile)] = value.astype(BF16)
-
-        return sink
-
-    @pl.when(z == 0)
-    def _():
-        for block in range(last, 0, -1):
-            sums(block, into(up_out, block))
-            up_copy(block).start()
-
-    @pl.when(z == last)
-    def _():
-        for block in range(last):
-            sums(block, into(dn_out, block))
-            dn_copy(block).start()
-
-    for block in range(line):
+        lax.fori_loop(0, chunk // tile, body, 0)
+
+    def up_copy(c, block, where=above):
+        return remote(
+            up_out.at[c, block], up_in.at[c, block], up_send.at[c, block], up_recv.at[c, block],
+            where,
+        )
+
+    def dn_copy(c, block, where=below):
+        return remote(
+            dn_out.at[c, block], dn_in.at[c, block], dn_send.at[c, block], dn_recv.at[c, block],
+            where,
+        )
+
+    for c in range(chunks):
+        part(c)
+
+        @pl.when(z == 0)
+        def _():
+            for block in range(last, 0, -1):
+                up_out[c, block] = parts[c, block].astype(BF16)
+                up_copy(c, block).start()
+
+        @pl.when(z == last)
+        def _():
+            for block in range(last):
+                dn_out[c, block] = parts[c, block].astype(BF16)
+                dn_copy(c, block).start()
+
+    for k in range(1, line):
+        src = lax.rem(z + line - k, line)
         remote(
-            w_all.at[block, x], w_all.at[block, 1 - x], wx_send.at[block], wx_recv.at[block], side
+            pg_z.at[z], pg_a.at[src], pa_send.at[k], pa_recv.at[k], {"fsdp": 2 * src + x}
         ).wait_recv()
-
-    turned = proj_grad.astype(F32).T.astype(BF16)
+    xa_pass(3)
+    mine_a = jnp.concatenate([pg_a[b, x] for b in range(line)], axis=1)
+    side_a = jnp.concatenate([pg_a[b, 1 - x] for b in range(line)], axis=1)
+    all_a = jnp.concatenate([mine_a, side_a], axis=0)
+
+    def gathered(i, carry):
+        at = pl.multiple_of(i * tile, tile)
+        tokens = xa[:, :, pl.ds(at, tile)].reshape(line * rows, tile)
+        value = times(all_a, tokens, (1, 0))
+        wg_ref[:, pl.ds(at, tile)] = value[:width]
+        side_out[:, pl.ds(at, tile)] = value[width:].astype(BF16)
+        return carry
+
+    lax.fori_loop(0, wide // tile, gathered, 0)
+    side_copy = remote(side_out, side_in, side_sem.at[0], side_sem.at[1], side)
+    side_copy.start()
+
+    def relay(c):
+        for k in range(last):
+            up_block, dn_block = last - k, k
+
+            @pl.when(jnp.logical_and(z > 0, z < up_block))
+            def _():
+                up_copy(c, up_block, below).wait_recv()
+                up_out[c, up_block] = (
+                    parts[c, up_block] + up_in[c, up_block].astype(F32)
+                ).astype(BF16)
+                up_copy(c, up_block).start()
+
+            @pl.when(jnp.logical_and(z < last, z > dn_block))
+            def _():
+                dn_copy(c, dn_block, above).wait_recv()
+                dn_out[c, dn_block] = (
+                    parts[c, dn_block] + dn_in[c, dn_block].astype(F32)
+                ).astype(BF16)
+                dn_copy(c, dn_block).start()
 
     def back(i, carry):
         at = pl.multiple_of(i * tile, tile)
@@ -384,84 +474,68 @@
         ).astype(BF16)
         return carry
 
-    @pl.when(jnp.logical_or(z == 0, z == last))
-    def _():
-        lax.fori_loop(0, inner // tile, back, 0)
-
-    for k in range(last):
-        up_block, dn_block = last - k, k
-
-        @pl.when(jnp.logical_and(z > 0, z < up_block))
-        def _():
-            dn = remote(
-                up_out.at[up_block], up_in.at[up_block], up_send.at[up_block],
-                up_recv.at[up_block], below,
+    for c in range(chunks):
+        relay(c)
+    for block in range(line):
+        remote(
+            w_all.at[block, x], w_all.at[block, 1 - x], wx_send.at[block], wx_recv.at[block], side
+        ).wait_recv()
+    lax.fori_loop(0, inner // tile, back, 0)
+    side_copy.wait_recv()
+    wg_ref[:, :wide] = wg_ref[:, :wide] + side_in[...].astype(F32)
+    for c in range(chunks):
+        lanes = slice(wide + c * chunk, wide + (c + 1) * chunk)
+
+        @pl.when(z > 0)
+        def _():
+            up_copy(c, z, below).wait_recv()
+
+        @pl.when(z < last)
+        def _():
+            dn_copy(c, z, above).wait_recv()
+
+        @pl.when(z == 0)
+        def _():
+            wg_ref[:, lanes] = parts[c, z] + dn_in[c, z].astype(F32)
+
+        @pl.when(z == last)
+        def _():
+            wg_ref[:, lanes] = parts[c, z] + up_in[c, z].astype(F32)
+
+        @pl.when(jnp.logical_and(z > 0, z < last))
+        def _():
+            wg_ref[:, lanes] = (
+                parts[c, z] + up_in[c, z].astype(F32) + dn_in[c, z].astype(F32)
             )
-            dn.wait_recv()
-            sums(up_block, into(up_out, up_block), up_in)
-            up_copy(up_block).start()
-
-        @pl.when(jnp.logical_and(z < last, z > dn_block))
-        def _():
-            up = remote(
-                dn_out.at[dn_block], dn_in.at[dn_block], dn_send.at[dn_block],
-                dn_recv.at[dn_block], above,
-            )
-            up.wait_recv()
-            sums(dn_block, into(dn_out, dn_block), dn_in)
-            dn_copy(dn_block).start()
-
-    @pl.when(jnp.logical_and(z > 0, z < last))
-    def _():
-        lax.fori_loop(0, inner // tile, back, 0)
-
-    def final(at, value):
-        wg_ref[:, pl.ds(at, tile)] = value
-
-    def from_below():
-        remote(up_out.at[z], up_in.at[z], up_send.at[z], up_recv.at[z], below).wait_recv()
-
-    def from_above():
-        remote(dn_out.at[z], dn_in.at[z], dn_send.at[z], dn_recv.at[z], above).wait_recv()
-
-    @pl.when(z == 0)
-    def _():
-        from_above()
-        sums(z, final, dn_in)
-
-    @pl.when(z == last)
-    def _():
-        from_below()
-        sums(z, final, up_in)
-
-    @pl.when(jnp.logical_and(z > 0, z < last))
-    def _():
-        from_below()
-        from_above()
-        sums(z, final, up_in, dn_in)
-
-    for copy in (x_copy, ret_copy, tp_copy, ds_copy, raw_copy, pg_copy):
+
+    for copy in (x_copy, ret_copy, tp_copy, ds_copy, raw_copy, pg_copy, side_copy):
         copy.wait_send()
     for block in range(line):
         pj_copy(block).wait_send()
         w_side(block).wait_send()
 
-        @pl.when(block > z)
-        def _():
-            up_copy(block).wait_send()
-
-        @pl.when(block < z)
-        def _():
-            dn_copy(block).wait_send()
+        for c in range(chunks):
+            @pl.when(block > z)
+            def _():
+                up_copy(c, block).wait_send()
+
+            @pl.when(block < z)
+            def _():
+                dn_copy(c, block).wait_send()
+
+    for k in range(1, line):
+        pa_copy(k).wait_send()
 
     for s in range(line - 1):
         @pl.when(jnp.logical_and(z < last, z - s >= 0))
         def _():
             w_up(z - s, s).wait_send()
+            xa_up_copy(z - s, s).wait_send()
 
         @pl.when(jnp.logical_and(z > 0, z + s <= last))
         def _():
             w_dn(z + s, s).wait_send()
+            xa_dn_copy(z + s, s).wait_send()
 
 
 def fused_device(saved_inputs, returned, proj_weight, log_rate, step_bias, skip_gain):
@@ -472,6 +546,8 @@
     line = lax.axis_size("fsdp") // 2
     columns = line * 2 * width
     groups = heads // GROUP
+    wide = inner // 2
+    chunks, chunk = 2, (inner - wide) // 2
     vmem = pl.BlockSpec(memory_space=pltpu.VMEM)
     dma = pltpu.SemaphoreType.DMA
     grad_out, share = pl.pallas_call(
@@ -480,9 +556,17 @@
             jax.ShapeDtypeStruct((rows, inner), BF16),
             jax.ShapeDtypeStruct((width, inner), F32),
         ),
-        in_specs=[vmem] * 6,
+        in_specs=[pl.BlockSpec(memory_space=pl.ANY)] * 3 + [vmem] * 3,
         out_specs=(vmem, vmem),
         scratch_shapes=[
+            pltpu.VMEM((rows, inner), BF16),
+            pltpu.VMEM((groups, GROUP, rows), F32),
+            pltpu.VMEM((line, rows, wide), BF16),
+            pltpu.VMEM((line, 2, width, rows), BF16),
+            pltpu.VMEM((line, 2, width, rows), BF16),
+            pltpu.VMEM((chunks, line, width, chunk), F32),
+            pltpu.VMEM((width, wide), BF16),
+            pltpu.VMEM((width, wide), BF16),
             pltpu.VMEM((rows, inner), BF16),
             pltpu.VMEM((rows, inner), BF16),
             pltpu.VMEM((line, 2, width, inner), BF16),
@@ -501,24 +585,26 @@
             pltpu.VMEM((rows, inner), F32),
             pltpu.VMEM((2, line, width, rows), BF16),
             pltpu.VMEM((line, width, rows), BF16),
-            pltpu.VMEM((line, width, inner), BF16),
-            pltpu.VMEM((line, width, inner), BF16),
-            pltpu.VMEM((line, width, inner), BF16),
-            pltpu.VMEM((line, width, inner), BF16),
-            dma, dma((2,)), dma((2,)), dma((line,)), dma((line,)), dma((line,)),
+            pltpu.VMEM((chunks, line, width, chunk), BF16),
+            pltpu.VMEM((chunks, line, width, chunk), BF16),
+            pltpu.VMEM((chunks, line, width, chunk), BF16),
+            pltpu.VMEM((chunks, line, width, chunk), BF16),
+            dma, dma, dma, dma((line,)), dma((line,)), dma((line,)), dma((line,)), dma((line,)), dma((2,)),
+            dma((2,)), dma((2,)), dma((line,)), dma((line,)), dma((line,)),
             dma((line,)), dma((line,)), dma((line,)), dma((line,)), dma((2,)), dma((2,)),
-            dma((2,)), dma((2,)), dma((line,)), dma((line,)), dma((line,)), dma((line,)),
+            dma((2,)), dma((2,)), dma((chunks, line)), dma((chunks, line)), dma((chunks, line)),
+            dma((chunks, line)),
         ],
         compiler_params=pltpu.CompilerParams(
-            collective_id=0, has_side_effects=True, vmem_limit_bytes=48 * 1024 * 1024
+            collective_id=0, has_side_effects=True, vmem_limit_bytes=60 * 1024 * 1024
         ),
     )(
         inputs,
         returned[0],
         proj_weight[0].T,
-        log_rate[0][:, None],
-        step_bias[0][:, None],
-        jnp.repeat(skip_gain[0], HEAD_DIM)[None, :],
+        log_rate,
+        step_bias,
+        skip_gain,
     )
     return (grad_out[None], share.T[None])
 

time: 192 us -> 140 us (0.73)
  Pallas kernels: 183 us -> 136 us
  local copies, waits for them, and re-layouts: 7.86 us -> 3.45 us
    pallas_call x1, Pallas kernels: 183 us -> 136 us  [fused_device(): pl.pallas_call(functools.partial(fused_kernel, line, lax.axis_size('pp'))...]
    unnamed x8 -> x4, local copies, waits for them, and re-layouts: 5.56 us -> 3.45 us
where the time goes in v2:
time: 140 us
  Pallas kernels  136 us (97%)
  local copies, waits for them, and re-layouts  3.45 us (2%)
    pallas_call x1, Pallas kernels, fused_device(): pl.pallas_call(functools.partial(fused_kernel, line, lax.axis_size('pp'))...  136 us
    unnamed x4, local copies, waits for them, and re-layouts  3.45 us

profile of v2, /device:TPU:0, one launch (start us, length us, event | category | flops | bytes accessed | tf_op | source)
XLA Modules:
  0.0 139.9 jit_solution(815121080767327326)
XLA Ops:
  0.6 135.8 %shard_map.77 = (bf16[128,4096]{1,0:T(8,128)(2,1)}, f32[80,4096]{1,0:T(8,128)}) custom-call(bf16[128,4096]{1,0:T(8,128)(2,1)} %bitcast.10, bf16[128,4096]{1,0:T(8,128)(2,1)} %bitcast.11, bf16[80,4096]{1,0:T(8,128)(2,1)} %bitcast.13, f32[1,64]{1,0:T(1,128)} %rate_ref.1, f32[1,64]{1,0:T(1,128)} %bias_ref.1, f32[1,64]{1,0:T(1,128)} %gain_ref.1), custom_call_target="tpu_custom_call" | custom-call | tf_op jit(solution)/shard_map/pallas_call | solution.py:553
  136.4 0.0 copy-start
  136.4 2.4 %copy.10 = bf16[1,128,4096]{2,1,0:T(8,128)(2,1)} copy(bf16[1,128,4096]{2,1,0:T(8,128)(2,1)} %bitcast.12) | data formatting | bytes 2097152
  138.8 0.0 copy-done
  138.8 1.1 copy.11
Async XLA Ops:
  136.4 2.4 %copy-start = (f32[80,4096]{1,0:T(8,128)S(1)}, f32[80,4096]{1,0:T(8,128)}, u32[]{:S(2)}) copy-start(f32[80,4096]{1,0:T(8,128)} %get-tuple-element.5) | copy-start | bytes 3932164

commit v3 on v2

--- a/solution.py
+++ b/solution.py
@@ -125,7 +125,7 @@
     out_ref, wg_ref,
     x_ref, gain_s, xa, pg_z, pg_a, parts, side_out, side_in,
     arrived, x_other, w_all, proj, proj_tp, proj_theirs, projs,
-    dt_s, cum_s, ddt_s, rs_s, ds_s, ds_in, raw_out, raw_in, gx,
+    shift_s, cum_s, dshift_s, rs_s, ds_s, ds_in, raw_out, raw_in, gx,
     pg_x, pg_in, up_out, dn_out, up_in, dn_in,
     local_sem, local_x, local_a, xa_recv, xa_up, xa_dn, pa_send, pa_recv, side_sem, ret_sem, x_sem, wz_recv, wz_up, wz_dn, wx_send, wx_recv,
     pj_send, pj_recv, tp_sem, ds_sem, raw_sem, pg_sem, up_send, up_recv, dn_send, dn_recv,
@@ -205,13 +205,32 @@
         pj_copy(block).start()
         proj[block, x] = times(weight, x_ref[...], (1, 1))
 
-    own_w.wait()
-    own_x.wait()
-    own_a.wait()
-    x_copy.wait_recv()
-    w_side(z).start()
-    project(z)
-    for s in range(1, line):
+    def xa_up_copy(block, s):
+        return remote(xa.at[block], xa.at[block], xa_up.at[s], xa_recv.at[block], above)
+
+    def xa_dn_copy(block, s):
+        return remote(xa.at[block], xa.at[block], xa_dn.at[s], xa_recv.at[block], below)
+
+    def xa_pass(s):
+        low, high = z - s, z + s
+
+        @pl.when(low >= 0)
+        def _():
+            xa_dn_copy(low, s - 1).wait_recv()
+            if s < line - 1:
+                @pl.when(z < last)
+                def _():
+                    xa_up_copy(low, s).start()
+
+        @pl.when(high <= last)
+        def _():
+            xa_up_copy(high, s - 1).wait_recv()
+            if s < line - 1:
+                @pl.when(z > 0)
+                def _():
+                    xa_dn_copy(high, s).start()
+
+    def w_pass(s):
         low, high = z - s, z + s
 
         @pl.when(low >= 0)
@@ -221,7 +240,6 @@
                 @pl.when(z < last)
                 def _():
                     w_up(low, s).start()
-            project(low)
 
         @pl.when(high <= last)
         def _():
@@ -230,36 +248,37 @@
                 @pl.when(z > 0)
                 def _():
                     w_dn(high, s).start()
-            project(high)
-
-    def xa_up_copy(block, s):
-        return remote(xa.at[block], xa.at[block], xa_up.at[s], xa_recv.at[block], above)
-
-    def xa_dn_copy(block, s):
-        return remote(xa.at[block], xa.at[block], xa_dn.at[s], xa_recv.at[block], below)
-
-    def xa_pass(s):
-        low, high = z - s, z + s
-
-        @pl.when(low >= 0)
-        def _():
-            if s > 0:
-                xa_dn_copy(low, s - 1).wait_recv()
-            if s < line - 1:
-                @pl.when(z < last)
-                def _():
-                    xa_up_copy(low, s).start()
-
-        @pl.when(high <= last)
-        def _():
-            if s > 0:
-                xa_up_copy(high, s - 1).wait_recv()
-            if s < line - 1:
-                @pl.when(z > 0)
-                def _():
-                    xa_dn_copy(high, s).start()
-
-    xa_pass(0)
+
+        @pl.when(jnp.logical_and(z == s - 1, z < last))
+        def _():
+            xa_up_copy(z, 0).start()
+
+        @pl.when(jnp.logical_and(z == last + 1 - s, z > 0))
+        def _():
+            xa_dn_copy(z, 0).start()
+
+    def project_at(s):
+        @pl.when(z - s >= 0)
+        def _():
+            project(z - s)
+
+        @pl.when(z + s <= last)
+        def _():
+            project(z + s)
+
+    own_w.wait()
+    own_x.wait()
+    own_a.wait()
+    w_pass(1)
+    x_copy.wait_recv()
+    w_side(z).start()
+    project(z)
+    w_pass(2)
+    project_at(1)
+    for s in range(3, line):
+        w_pass(s)
+        project_at(s - 1)
+    project_at(line - 1)
     for block in range(line):
         remote(
             proj_theirs.at[block], proj.at[block, 1 - x], pj_send.at[block], pj_recv.at[block], side
@@ -274,8 +293,8 @@
 
     row_at = lax.broadcasted_iota(jnp.int32, (rows, rows), 0)
     column_at = lax.broadcasted_iota(jnp.int32, (rows, rows), 1)
-    causal = row_at >= column_at
-    lower = causal.astype(F32)
+    lower = (row_at >= column_at).astype(F32)
+    causal = row_at <= column_at
     upper = (row_at <= column_at).astype(F32)
     b_t, c_t = projs[:STATE], projs[STATE : 2 * STATE]
     start = pl.multiple_of(2 * STATE + tp * heads, 8)
@@ -284,9 +303,13 @@
     decay = -jnp.exp(jnp.broadcast_to(rate_ref[...], (rows, heads)).T)
     groups = heads // GROUP
     gain_s[...] = jnp.broadcast_to(gain_ref[...], (rows, heads)).T.reshape(groups, GROUP, rows)
-    cum_s[...] = times(step * decay, upper, (1, 0), exact).reshape(groups, GROUP, rows)
-    dt_s[...] = step.reshape(groups, GROUP, rows)
-    scores = times(c_t, b_t, (0, 0), exact)
+    cumulative = times(step * decay, upper, (1, 0), exact)
+    cum_s[...] = cumulative.reshape(groups, GROUP, rows)
+    shift_s[...] = (cumulative - jnp.log(step)).reshape(groups, GROUP, rows)
+    head_of = lax.broadcasted_iota(jnp.int32, (GROUP, GROUP * HEAD_DIM), 1) // HEAD_DIM
+    picks = (head_of == lax.broadcasted_iota(jnp.int32, head_of.shape, 0)).astype(F32).astype(BF16)
+    scores = times(b_t, c_t, (0, 0), exact)
+    scores = jnp.concatenate([scores, scores], axis=1)
     ds_s[...] = jnp.zeros_like(ds_s)
     pair_lanes = 2 * HEAD_DIM
     lane = lax.broadcasted_iota(jnp.int32, (rows, pair_lanes), 1)
@@ -294,20 +317,18 @@
 
     def group_step(g, carry):
         cum_rows = cum_s[g]
-        cum_columns = cum_rows.T
-        dt_rows = dt_s[g]
+        shift_columns = shift_s[g].T
         gain_rows = gain_s[g]
 
-        @pl.when(g == groups // 2)
+        @pl.when(g == groups // 4)
         def _():
             xa_pass(1)
 
-        ddt_rows, rs_columns = [], []
+        rs_rows, shares, ds_part = [], [], None
         for p in range(GROUP // 2):
             at = pl.multiple_of(g * (GROUP * HEAD_DIM) + p * pair_lanes, pair_lanes)
-            g_pair = arrived[:, pl.ds(at, pair_lanes)]
+            g_wide = arrived[:, pl.ds(at, pair_lanes)].astype(F32)
             x_pair = x_ref[:, pl.ds(at, pair_lanes)]
-            g_wide = g_pair.astype(F32)
             g_both = jnp.concatenate(
                 [
                     jnp.where(lane < HEAD_DIM, g_wide, 0.0).astype(BF16),
@@ -315,45 +336,48 @@
                 ],
                 axis=0,
             )
-            products = times(g_both, x_pair, (1, 1))
-            mixed, ds_part = [], None
-            for e in range(2):
-                h = 2 * p + e
-                dt_row = dt_rows[h : h + 1]
-                gap = cum_columns[:, h : h + 1] - cum_rows[h : h + 1]
-                mask = jnp.exp(jnp.where(causal, gap, -1e30))
-                product = products[e * rows : (e + 1) * rows]
-                with_scores = mask * scores
-                total = with_scores * product
-                ddt_rows.append(jnp.sum(total, axis=0, keepdims=True))
-                rs_columns.append(jnp.sum(total * dt_row, axis=1, keepdims=True))
-                part = mask * product * dt_row
-                ds_part = part if ds_part is None else ds_part + part
-                mixed.append((with_scores * dt_row).astype(BF16))
-            ds_s[...] += ds_part
-            dx = times(jnp.concatenate(mixed, axis=0), g_both, (0, 0))
+            products = times(x_pair, g_both, (1, 1))
+            masks = []
+            for h in (2 * p, 2 * p + 1):
+                gap = cum_rows[h : h + 1] - shift_columns[:, h : h + 1]
+                masks.append(jnp.exp(jnp.where(causal, gap, -1e30)))
+            mask = jnp.concatenate(masks, axis=1)
+            mixed = mask * scores
+            sums = jnp.sum(mixed * products, axis=0, keepdims=True)
+            rs_rows += [sums[:, :rows], sums[:, rows:]]
+            weighted = mask * products
+            weighted = weighted[:, :rows] + weighted[:, rows:]
+            ds_part = weighted if ds_part is None else ds_part + weighted
+            dx = times(mixed.astype(BF16), g_both, (1, 0))
             gain = jnp.where(
                 lane[:1] < HEAD_DIM, gain_rows[2 * p : 2 * p + 1], gain_rows[2 * p + 1 : 2 * p + 2]
             )
             gx[:, pl.ds(at, pair_lanes)] = dx + (1.0 + gain) * g_wide
-        ddt_s[g] = jnp.concatenate(ddt_rows, axis=0)
-        rs_s[g] = jnp.concatenate(rs_columns, axis=1).T
+            shares.append(dx * x_pair.astype(F32))
+        ds_s[...] += ds_part
+        share = jnp.concatenate(shares, axis=1)
+        high = share.astype(BF16)
+        low = (share - high.astype(F32)).astype(BF16)
+        dshift_s[g] = times(picks, high, (1, 1)) + times(picks, low, (1, 1))
+        rs_s[g] = jnp.concatenate(rs_rows, axis=0)
         return carry
 
     lax.fori_loop(0, groups, group_step, 0)
     ds_copy = remote(ds_s, ds_in, ds_sem.at[0], ds_sem.at[1], core)
     ds_copy.start()
     xa_pass(2)
-    ddt = ddt_s[...].reshape(heads, rows)
-    d_cum = rs_s[...].reshape(heads, rows) - step * ddt
+    ddt = dshift_s[...].reshape(heads, rows)
+    d_cum = rs_s[...].reshape(heads, rows) - ddt
     d_decay = times(d_cum, lower, (1, 0), exact)
-    raw_out[...] = ((ddt + d_decay * decay) * (1.0 / (1.0 + jnp.exp(-raw)))).astype(BF16)
+    slope = jnp.exp(jnp.minimum(raw, 0.0)) / (1.0 + jnp.exp(-jnp.abs(raw)))
+    ratio = jnp.where(step > 1e-30, slope / jnp.maximum(step, 1e-30), 1.0)
+    raw_out[...] = (ddt * ratio + d_decay * decay * slope).astype(BF16)
     raw_copy = remote(raw_out, raw_in, raw_sem.at[0], raw_sem.at[1], core)
     raw_copy.start()
     ds_copy.wait_recv()
     ds_total = ds_s[...] + ds_in[...]
-    grad_b = times(c_t, ds_total, (1, 0), exact).astype(BF16)
-    grad_c = times(b_t, ds_total, (1, 1), exact).astype(BF16)
+    grad_b = times(c_t, ds_total, (1, 1), exact).astype(BF16)
+    grad_c = times(b_t, ds_total, (1, 0), exact).astype(BF16)
     raw_copy.wait_recv()
     mine, other = raw_out[...].astype(F32), raw_in[...].astype(F32)
     first = jnp.where(tp == 0, mine, other).astype(BF16)

time: 140 us -> 130 us (0.929)
  Pallas kernels: 136 us -> 126 us
    pallas_call x1, Pallas kernels: 136 us -> 126 us  [fused_device(): pl.pallas_call(functools.partial(fused_kernel, line, lax.axis_size('pp'))...]
where the time goes in v3:
time: 130 us
  Pallas kernels  126 us (97%)
  local copies, waits for them, and re-layouts  3.45 us (3%)
    pallas_call x1, Pallas kernels, fused_device(): pl.pallas_call(functools.partial(fused_kernel, line, lax.axis_size('pp'))...  126 us
    unnamed x4, local copies, waits for them, and re-layouts  3.45 us

profile of v3, /device:TPU:0, one launch (start us, length us, event | category | flops | bytes accessed | tf_op | source)
XLA Modules:
  0.0 130.1 jit_solution(15109729319963201368)
XLA Ops:
  0.6 126.0 %shard_map.77 = (bf16[128,4096]{1,0:T(8,128)(2,1)}, f32[80,4096]{1,0:T(8,128)}) custom-call(bf16[128,4096]{1,0:T(8,128)(2,1)} %bitcast.10, bf16[128,4096]{1,0:T(8,128)(2,1)} %bitcast.11, bf16[80,4096]{1,0:T(8,128)(2,1)} %bitcast.13, f32[1,64]{1,0:T(1,128)} %rate_ref.1, f32[1,64]{1,0:T(1,128)} %bias_ref.1, f32[1,64]{1,0:T(1,128)} %gain_ref.1), custom_call_target="tpu_custom_call" | custom-call | tf_op jit(solution)/shard_map/pallas_call | solution.py:577
  126.7 0.0 copy-start
  126.7 2.4 %copy.10 = bf16[1,128,4096]{2,1,0:T(8,128)(2,1)} copy(bf16[1,128,4096]{2,1,0:T(8,128)(2,1)} %bitcast.12) | data formatting | bytes 2097152
  129.1 0.0 copy-done
  129.1 1.1 copy.11
Async XLA Ops:
  126.7 2.4 %copy-start = (f32[80,4096]{1,0:T(8,128)S(1)}, f32[80,4096]{1,0:T(8,128)}, u32[]{:S(2)}) copy-start(f32[80,4096]{1,0:T(8,128)} %get-tuple-element.5) | copy-start | bytes 3932164

commit v4 on v3

--- a/solution.py
+++ b/solution.py
@@ -123,11 +123,11 @@
     line, pairs,
     x_hbm, ret_ref, w_ref, rate_ref, bias_ref, gain_ref,
     out_ref, wg_ref,
-    x_ref, gain_s, xa, pg_z, pg_a, parts, side_out, side_in,
+    x_ref, gain_s, xa, pg_z, pg_a, parts, side_out, side_in, bp_out, bp_in,
     arrived, x_other, w_all, proj, proj_tp, proj_theirs, projs,
     shift_s, cum_s, dshift_s, rs_s, ds_s, ds_in, raw_out, raw_in, gx,
     pg_x, pg_in, up_out, dn_out, up_in, dn_in,
-    local_sem, local_x, local_a, xa_recv, xa_up, xa_dn, pa_send, pa_recv, side_sem, ret_sem, x_sem, wz_recv, wz_up, wz_dn, wx_send, wx_recv,
+    local_sem, local_x, local_a, xa_recv, xa_up, xa_dn, pa_send, pa_recv, side_sem, bp_sem, ret_sem, x_sem, wz_recv, wz_up, wz_dn, wx_send, wx_recv,
     pj_send, pj_recv, tp_sem, ds_sem, raw_sem, pg_sem, up_send, up_recv, dn_send, dn_recv,
 ):
     exact = lax.Precision.HIGHEST
@@ -173,10 +173,9 @@
         src = w_ref if s == 0 else w_all.at[block, x]
         return remote(src, w_all.at[block, x], wz_dn.at[s], wz_recv.at[block], below)
 
-    def w_side(block):
-        return remote(
-            w_all.at[block, x], w_all.at[block, x], wx_send.at[block], wx_recv.at[block], side
-        )
+    def w_side(block, column=x):
+        half = w_all.at[block, column, :, pl.ds(0, wide)]
+        return remote(half, half, wx_send.at[block], wx_recv.at[block], side)
 
     @pl.when(z < last)
     def _():
@@ -273,6 +272,11 @@
     x_copy.wait_recv()
     w_side(z).start()
     project(z)
+    for low_or_high in (z - 1, z + 1):
+        @pl.when(jnp.logical_and(low_or_high >= 0, low_or_high <= last))
+        def _():
+            w_side(low_or_high).start()
+
     w_pass(2)
     project_at(1)
     for s in range(3, line):
@@ -288,8 +292,10 @@
     tp_copy.wait_recv()
     projs[...] = (proj[...] + proj_tp[...]).reshape(projs.shape)
 
-    for k in range(1, line - 1):
-        w_side(lax.rem(z + k, line)).start()
+    for block in range(line):
+        @pl.when(jnp.logical_or(block > z + 1, block < z - 1))
+        def _():
+            w_side(block).start()
 
     row_at = lax.broadcasted_iota(jnp.int32, (rows, rows), 0)
     column_at = lax.broadcasted_iota(jnp.int32, (rows, rows), 1)
@@ -399,7 +405,6 @@
     turned = proj_grad.astype(F32).T.astype(BF16)
     pg_a[z] = pg_z[z]
     pg_copy.wait_recv()
-    w_side(lax.rem(z + line - 1, line)).start()
 
     tile = 512
     chunk = parts.shape[3]
@@ -421,6 +426,20 @@
 
         lax.fori_loop(0, chunk // tile, body, 0)
 
+    def turn(value):
+        return value.reshape(line * width, rows).astype(F32).T.astype(BF16)
+
+    bp_copy = remote(bp_out, bp_in, bp_sem.at[0], bp_sem.at[1], side)
+    turned_in = turn(pg_in[...])
+    turned_own = turn(pg_x[x])
+
+    def back_other(i, carry):
+        at = pl.multiple_of(i * tile, tile)
+        far = pl.multiple_of(wide + i * tile, tile)
+        weight = w_all[:, x, :, pl.ds(far, tile)].reshape(line * width, tile)
+        bp_out[:, pl.ds(at, tile)] = times(turned_in, weight, (1, 0)).astype(BF16)
+        return carry
+
     def up_copy(c, block, where=above):
         return remote(
             up_out.at[c, block], up_in.at[c, block], up_send.at[c, block], up_recv.at[c, block],
@@ -448,6 +467,8 @@
                 dn_out[c, block] = parts[c, block].astype(BF16)
                 dn_copy(c, block).start()
 
+    lax.fori_loop(0, (inner - wide) // tile, back_other, 0)
+    bp_copy.start()
     for k in range(1, line):
         src = lax.rem(z + line - k, line)
         remote(
@@ -501,10 +522,22 @@
     for c in range(chunks):
         relay(c)
     for block in range(line):
-        remote(
-            w_all.at[block, x], w_all.at[block, 1 - x], wx_send.at[block], wx_recv.at[block], side
-        ).wait_recv()
-    lax.fori_loop(0, inner // tile, back, 0)
+        w_side(block, 1 - x).wait_recv()
+    lax.fori_loop(0, wide // tile, back, 0)
+    bp_copy.wait_recv()
+
+    def back_far(i, carry):
+        at = pl.multiple_of(i * tile, tile)
+        far = pl.multiple_of(wide + i * tile, tile)
+        weight = w_all[:, x, :, pl.ds(far, tile)].reshape(line * width, tile)
+        out_ref[:, pl.ds(far, tile)] = (
+            gx[:, pl.ds(far, tile)]
+            + times(turned_own, weight, (1, 0))
+            + bp_in[:, pl.ds(at, tile)].astype(F32)
+        ).astype(BF16)
+        return carry
+
+    lax.fori_loop(0, (inner - wide) // tile, back_far, 0)
     side_copy.wait_recv()
     wg_ref[:, :wide] = wg_ref[:, :wide] + side_in[...].astype(F32)
     for c in range(chunks):
@@ -532,7 +565,7 @@
                 parts[c, z] + up_in[c, z].astype(F32) + dn_in[c, z].astype(F32)
             )
 
-    for copy in (x_copy, ret_copy, tp_copy, ds_copy, raw_copy, pg_copy, side_copy):
+    for copy in (x_copy, ret_copy, tp_copy, ds_copy, raw_copy, pg_copy, side_copy, bp_copy):
         copy.wait_send()
     for block in range(line):
         pj_copy(block).wait_send()
@@ -591,6 +624,8 @@
             pltpu.VMEM((chunks, line, width, chunk), F32),
             pltpu.VMEM((width, wide), BF16),
             pltpu.VMEM((width, wide), BF16),
+            pltpu.VMEM((rows, inner - wide), BF16),
+            pltpu.VMEM((rows, inner - wide), BF16),
             pltpu.VMEM((rows, inner), BF16),
             pltpu.VMEM((rows, inner), BF16),
             pltpu.VMEM((line, 2, width, inner), BF16),
@@ -613,7 +648,7 @@
             pltpu.VMEM((chunks, line, width, chunk), BF16),
             pltpu.VMEM((chunks, line, width, chunk), BF16),
             pltpu.VMEM((chunks, line, width, chunk), BF16),
-            dma, dma, dma, dma((line,)), dma((line,)), dma((line,)), dma((line,)), dma((line,)), dma((2,)),
+            dma, dma, dma, dma((line,)), dma((line,)), dma((line,)), dma((line,)), dma((line,)), dma((2,)), dma((2,)),
             dma((2,)), dma((2,)), dma((line,)), dma((line,)), dma((line,)),
             dma((line,)), dma((line,)), dma((line,)), dma((line,)), dma((2,)), dma((2,)),
             dma((2,)), dma((2,)), dma((chunks, line)), dma((chunks, line)), dma((chunks, line)),

time: 130 us -> 119 us (0.915)
  Pallas kernels: 126 us -> 114 us
    pallas_call x1, Pallas kernels: 126 us -> 114 us  [fused_device(): pl.pallas_call(functools.partial(fused_kernel, line, lax.axis_size('pp'))...]
where the time goes in v4:
time: 119 us; the launch traced here: 118 us
  Pallas kernels  114 us (96%)
  local copies, waits for them, and re-layouts  3.45 us (3%)
    pallas_call x1, Pallas kernels, fused_device(): pl.pallas_call(functools.partial(fused_kernel, line, lax.axis_size('pp'))...  114 us
    unnamed x4, local copies, waits for them, and re-layouts  3.45 us

profile of v4, /device:TPU:0, one launch (start us, length us, event | category | flops | bytes accessed | tf_op | source)
XLA Modules:
  0.0 118.4 jit_solution(9925728843434176422)
XLA Ops:
  0.6 114.3 %shard_map.77 = (bf16[128,4096]{1,0:T(8,128)(2,1)}, f32[80,4096]{1,0:T(8,128)}) custom-call(bf16[128,4096]{1,0:T(8,128)(2,1)} %bitcast.10, bf16[128,4096]{1,0:T(8,128)(2,1)} %bitcast.11, bf16[80,4096]{1,0:T(8,128)(2,1)} %bitcast.13, f32[1,64]{1,0:T(1,128)} %rate_ref.1, f32[1,64]{1,0:T(1,128)} %bias_ref.1, f32[1,64]{1,0:T(1,128)} %gain_ref.1), custom_call_target="tpu_custom_call" | custom-call | tf_op jit(solution)/shard_map/pallas_call | solution.py:610
  114.9 0.0 copy-start
  114.9 2.4 %copy.10 = bf16[1,128,4096]{2,1,0:T(8,128)(2,1)} copy(bf16[1,128,4096]{2,1,0:T(8,128)(2,1)} %bitcast.12) | data formatting | bytes 2097152
  117.3 0.0 copy-done
  117.3 1.1 copy.11
Async XLA Ops:
  114.9 2.4 %copy-start = (f32[80,4096]{1,0:T(8,128)S(1)}, f32[80,4096]{1,0:T(8,128)}, u32[]{:S(2)}) copy-start(f32[80,4096]{1,0:T(8,128)} %get-tuple-element.5) | copy-start | bytes 3932164

commit v5 on v4

--- a/solution.py
+++ b/solution.py
@@ -519,11 +519,13 @@
         ).astype(BF16)
         return carry
 
-    for c in range(chunks):
+    for c in range(chunks // 2):
         relay(c)
     for block in range(line):
         w_side(block, 1 - x).wait_recv()
     lax.fori_loop(0, wide // tile, back, 0)
+    for c in range(chunks // 2, chunks - 1):
+        relay(c)
     bp_copy.wait_recv()
 
     def back_far(i, carry):
@@ -538,6 +540,7 @@
         return carry
 
     lax.fori_loop(0, (inner - wide) // tile, back_far, 0)
+    relay(chunks - 1)
     side_copy.wait_recv()
     wg_ref[:, :wide] = wg_ref[:, :wide] + side_in[...].astype(F32)
     for c in range(chunks):
@@ -604,7 +607,8 @@
     columns = line * 2 * width
     groups = heads // GROUP
     wide = inner // 2
-    chunks, chunk = 2, (inner - wide) // 2
+    chunks = 4
+    chunk = (inner - wide) // chunks
     vmem = pl.BlockSpec(memory_space=pltpu.VMEM)
     dma = pltpu.SemaphoreType.DMA
     grad_out, share = pl.pallas_call(

time: 119 us -> 126 us (1.059)
  Pallas kernels: 114 us -> 121 us
    pallas_call x1, Pallas kernels: 114 us -> 121 us  [fused_device(): pl.pallas_call(functools.partial(fused_kernel, line, lax.axis_size('pp'))...]
where the time goes in v5:
time: 126 us; the launch traced here: 125 us
  Pallas kernels  121 us (96%)
  local copies, waits for them, and re-layouts  3.45 us (3%)
    pallas_call x1, Pallas kernels, fused_device(): pl.pallas_call(functools.partial(fused_kernel, line, lax.axis_size('pp'))...  121 us
    unnamed x4, local copies, waits for them, and re-layouts  3.45 us

profile of v5, /device:TPU:0, one launch (start us, length us, event | category | flops | bytes accessed | tf_op | source)
XLA Modules:
  0.0 125.4 jit_solution(12509431185315294007)
XLA Ops:
  0.6 121.3 %shard_map.77 = (bf16[128,4096]{1,0:T(8,128)(2,1)}, f32[80,4096]{1,0:T(8,128)}) custom-call(bf16[128,4096]{1,0:T(8,128)(2,1)} %bitcast.10, bf16[128,4096]{1,0:T(8,128)(2,1)} %bitcast.11, bf16[80,4096]{1,0:T(8,128)(2,1)} %bitcast.13, f32[1,64]{1,0:T(1,128)} %rate_ref.1, f32[1,64]{1,0:T(1,128)} %bias_ref.1, f32[1,64]{1,0:T(1,128)} %gain_ref.1), custom_call_target="tpu_custom_call" | custom-call | tf_op jit(solution)/shard_map/pallas_call | solution.py:614
  122.0 0.0 copy-start
  122.0 2.4 %copy.10 = bf16[1,128,4096]{2,1,0:T(8,128)(2,1)} copy(bf16[1,128,4096]{2,1,0:T(8,128)(2,1)} %bitcast.12) | data formatting | bytes 2097152
  124.4 0.0 copy-done
  124.4 1.1 copy.11
Async XLA Ops:
  122.0 2.4 %copy-start = (f32[80,4096]{1,0:T(8,128)S(1)}, f32[80,4096]{1,0:T(8,128)}, u32[]{:S(2)}) copy-start(f32[80,4096]{1,0:T(8,128)} %get-tuple-element.5) | copy-start | bytes 3932164
